TPU v7x, 32 devices: a whole 2x2x4 slice. The times are simulated.
32 devices in a mesh: leaf: 8 (over z, y), sub: 4 (over x, core).
Axes of the slice: x: 2, y: 2, z: 4, core: 2. Of those that a mesh axis runs over, the one named last changes fastest.
Arguments:
- sources: bfloat16 [32, 262144], P(None, ('leaf', 'sub')), may hold values from -6 to 6
- leaf_basis: bfloat16 [2048, 64, 128], P(('leaf', 'sub')), may hold values from -0.5 to 0.5
- near_blocks: bfloat16 [6144, 128, 128], P(('leaf', 'sub')), may hold values from -0.3125 to 0.3125
- near_index: int32 [6144, 2], P(('leaf', 'sub')), may hold values from 0 to 2047, as said below
- near_count: int32 [32], P(('leaf', 'sub')), may hold values from 96 to 192, as said below
- transfer: bfloat16 [4064, 4096], P(('leaf', 'sub')), may hold values from -0.5 to 0.5
- couple_first: bfloat16 [6144, 4096], P(('leaf', 'sub')), may hold values from -0.4375 to 0.4375
- couple_second: bfloat16 [3072, 4096], P(('leaf', 'sub')), may hold values from -0.4375 to 0.4375
- couple_third: bfloat16 [1536, 4096], P(('leaf', 'sub')), may hold values from -0.4375 to 0.4375
- index_first: int32 [6144, 2], P(('leaf', 'sub')), may hold values from 0 to 2047, as said below
- index_second: int32 [3072, 2], P(('leaf', 'sub')), may hold values from 0 to 1023, as said below
- index_third: int32 [1536, 2], P(('leaf', 'sub')), may hold values from 0 to 511, as said below
- couple_count: int32 [32, 3], P(('leaf', 'sub')), may hold values from 24 to 192, as said below
- fold_transfer: bfloat16 [16, 4096], replicated, may hold values from -0.5 to 0.5
- top_couple: bfloat16 [8, 8, 4096], P('leaf'), may hold values from -0.75 to 0.75
Outputs:
- potential: float32 [32, 262144], P(None, ('leaf', 'sub'))
Inputs may be any that keep to these rules, and one draw needn't show every extreme that they name: `near_index`: the slots of one device list each of its 64 leaves as row leaf 3 times, in the order of the leaves repeated; a slot's column leaf lies at most 16 leaves from its row leaf. Only the first near_count[d] slots of device d are live; some device has all its slots live. `index_first`: the slots of one device list each of its level-0 nodes as row node 3 times, in the order of the nodes repeated; a partner node lies 2 or 3 nodes from its row node. `index_second`: the slots of one device list each of its level-1 nodes as row node 3 times, in the order of the nodes repeated; a partner node lies 2 or 3 nodes from its row node. `index_third`: the slots of one device list each of its level-2 nodes as row node 3 times, in the order of the nodes repeated; a partner node lies 2 or 3 nodes from its row node. `couple_count`: column j counts the live slots of level j, at least half of them; at each level some device has all its slots live.
All inputs are finite; a program needn't handle non-finite values.
Results may differ from a plain program's by a relative error of at most 0.02.
Values may be sent and summed in bfloat16 or wider, within the bound.
A program may use at most 64 MiB of HBM per device.

v0:
```python
import jax
import jax.numpy as jnp
from jax import lax
from jax.sharding import PartitionSpec as P

REACH = 16
COUPLED = 3


highest = lax.Precision.HIGHEST


def with_halo(block, sides, width):
    for axis, dim in sides:
        count = lax.axis_size(axis)
        forward = [(i, i + 1) for i in range(count - 1)]
        backward = [(target, source) for source, target in forward]
        low = lax.ppermute(
            lax.slice_in_dim(block, block.shape[dim] - width, None, axis=dim), axis, forward
        )
        high = lax.ppermute(lax.slice_in_dim(block, 0, width, axis=dim), axis, backward)
        block = jnp.concatenate([low, block, high], axis=dim)
    return block


def fold_upward(terms, fold_mats):
    columns, groups, members, rank_size = terms.shape
    current = terms.reshape(columns, groups, members // 2, 2, rank_size).sum(3).astype(jnp.bfloat16)
    kept_levels = [current]
    offset = 0
    members = members // 2
    while members > 1:
        products = jnp.einsum(
            "rgnk,gnkm->rgnm", current, fold_mats, preferred_element_type=jnp.float32
        )
        offset = offset + members
        current = (
            products.reshape(columns, groups, members // 2, 2, rank_size)
            .sum(3)
            .astype(jnp.bfloat16)
        )
        kept_levels.append(current)
        members = members // 2
    return kept_levels


def fold_downward(top_field, fold_mats, members):
    current = top_field
    node_count = 2
    while node_count <= members // 2:
        expanded = jnp.repeat(current.astype(jnp.bfloat16), 2, axis=2)
        current = jnp.einsum(
            "rgnm,gnkm->rgnk", expanded, fold_mats, preferred_element_type=jnp.float32
        )
        node_count = node_count * 2
    return current


def couple_level(padded, matrices, indices, live_count, device, node_count):
    slot_count = matrices.shape[0]
    rank_size = padded.shape[2]
    first_node = device * node_count - 3
    picked = jnp.take(padded, indices[:, 1] - first_node, axis=1)
    products = jnp.einsum(
        "rsk,skm->rsm",
        picked,
        matrices.reshape(slot_count, rank_size, rank_size),
        preferred_element_type=jnp.float32,
    )
    live_mask = jnp.where(lax.iota(jnp.int32, slot_count) < live_count, 1.0, 0.0).astype(
        jnp.float32
    )
    products = products * live_mask[None, :, None]
    return products.reshape(products.shape[0], slot_count // node_count, node_count, rank_size).sum(
        1
    )


def local(
    sources,
    leaf_basis,
    near_blocks,
    near_index,
    near_count,
    transfer,
    couple_first,
    couple_second,
    couple_third,
    index_first,
    index_second,
    index_third,
    couple_count,
    fold_transfer,
    top_couple,
):
    columns = sources.shape[0]
    per_device, rank_size, leaf_size = leaf_basis.shape
    near_slots = near_blocks.shape[0]
    device = lax.axis_index(("leaf", "sub"))
    leaf_group = lax.axis_index("leaf")
    sub_member = lax.axis_index("sub")
    groups = lax.axis_size("leaf")
    members = lax.axis_size("sub")
    local_sources = sources.reshape(columns, per_device, leaf_size)
    padded_sources = with_halo(sources, ((("leaf", "sub"), 1),), REACH * leaf_size).reshape(
        columns, per_device + 2 * REACH, leaf_size
    )
    picked = jnp.take(padded_sources, near_index[:, 1] - (device * per_device - REACH), axis=1)
    near_products = jnp.einsum(
        "bij,rbj->rbi", near_blocks, picked, preferred_element_type=jnp.float32
    )
    near_live = jnp.where(lax.iota(jnp.int32, near_slots) < near_count[0], 1.0, 0.0).astype(
        jnp.float32
    )
    near_products = near_products * near_live[None, :, None]
    near_field = near_products.reshape(
        columns, near_slots // per_device, per_device, leaf_size
    ).sum(1)
    tree_depth = per_device.bit_length() - 1

    def level_mats(level_no):
        node_count = per_device >> level_no
        start_row = 2 * per_device - 2 * node_count
        return transfer[start_row : start_row + node_count].reshape(
            node_count, rank_size, rank_size
        )

    couples = (
        (couple_first, index_first),
        (couple_second, index_second),
        (couple_third, index_third),
    )
    levels = [
        jnp.einsum(
            "lkp,rlp->rlk", leaf_basis, local_sources, preferred_element_type=jnp.float32
        ).astype(jnp.bfloat16)
    ]
    fields = []
    for level_no in range(tree_depth):
        if level_no < COUPLED:
            padded = with_halo(levels[level_no], ((("leaf", "sub"), 1),), 3)
            fields.append(
                couple_level(
                    padded,
                    couples[level_no][0],
                    couples[level_no][1],
                    couple_count[0, level_no],
                    device,
                    per_device >> level_no,
                )
            )
        products = jnp.einsum(
            "rnk,nkm->rnm",
            levels[level_no],
            level_mats(level_no),
            preferred_element_type=jnp.float32,
        )
        levels.append(products.reshape(columns, -1, 2, rank_size).sum(2).astype(jnp.bfloat16))
    top_terms = jnp.einsum(
        "rnk,nkm->rnm",
        levels[tree_depth],
        level_mats(tree_depth),
        preferred_element_type=jnp.float32,
    )
    fold_mats = fold_transfer.reshape(groups, members - 2, rank_size, rank_size)
    own_mats = lax.dynamic_slice_in_dim(fold_mats, leaf_group, 1, 0)
    group_terms = lax.all_gather(top_terms, "sub", axis=1, tiled=True)
    kept_levels = fold_upward(group_terms[:, None], own_mats)
    top_coeffs = lax.all_gather(kept_levels[-1][:, 0], "leaf", axis=1, tiled=True)
    top_mats = top_couple.reshape(groups, rank_size, rank_size)
    top_products = jnp.einsum(
        "rjk,jkm->rjm", top_coeffs, top_mats, preferred_element_type=jnp.float32
    )
    distance = jnp.abs(lax.iota(jnp.int32, groups) - leaf_group)
    far_mask = jnp.where(distance >= 2, 1.0, 0.0).astype(jnp.float32)
    top_field = jnp.einsum("rjm,j->rm", top_products, far_mask, precision=highest)
    down_field = fold_downward(top_field[:, None, None, :], own_mats, members)[:, 0]
    parent_node = lax.dynamic_slice_in_dim(down_field, sub_member // 2, 1, 1).astype(jnp.bfloat16)
    down_field = jnp.einsum(
        "rnm,nkm->rnk", parent_node, level_mats(tree_depth), preferred_element_type=jnp.float32
    )
    for level_no in reversed(range(tree_depth)):
        expanded = jnp.repeat(down_field.astype(jnp.bfloat16), 2, axis=1)
        down_field = jnp.einsum(
            "rnm,nkm->rnk", expanded, level_mats(level_no), preferred_element_type=jnp.float32
        )
        if level_no < COUPLED:
            down_field = down_field + fields[level_no]
    far_field = jnp.einsum(
        "rlk,lkp->rlp",
        down_field.astype(jnp.bfloat16),
        leaf_basis,
        preferred_element_type=jnp.float32,
    )
    return (near_field + far_field).reshape(columns, per_device * leaf_size)


def solution(mesh):
    return jax.shard_map(
        local,
        mesh=mesh,
        in_specs=(
            P(None, ("leaf", "sub")),
            P(("leaf", "sub"), None, None),
            P(("leaf", "sub"), None, None),
            P(("leaf", "sub"), None),
            P(("leaf", "sub")),
            P(("leaf", "sub"), None),
            P(("leaf", "sub"), None),
            P(("leaf", "sub"), None),
            P(("leaf", "sub"), None),
            P(("leaf", "sub"), None),
            P(("leaf", "sub"), None),
            P(("leaf", "sub"), None),
            P(("leaf", "sub"), None),
            P(),
            P("leaf", None, None),
        ),
        out_specs=P(None, ("leaf", "sub")),
        check_vma=False,
    )
```

profile of v0, /device:TPU:0, one launch (start us, length us, event | category | flops | bytes accessed | tf_op | source)
XLA Modules:
  0.0 167.3 jit_solution(16382745042688231667)
XLA Ops:
  6.9 3.1 %collective-permute-start.2 = (bf16[32,3,64]{2,0,1:T(8,128)(2,1)}, bf16[32,3,64]{2,0,1:T(8,128)(2,1)}, u32[]{:S(2)}, u32[]{:S(2)}) collective-permute-start(bf16[32,3,64]{2,0,1:T(8,128)(2,1)} %get-tuple-element.19), channel_id=1, source_target_pairs={{0,1},{1,2},{2,3},{3,4},{4,5},{5,6},{6,7},{7,8},{8,9},{9,10},{10,1... | collective-permute-start | bytes 36872 | tf_op jit(solution)/shard_map/ppermute | solution.py:18
  11.9 5.2 %collective-permute-start.4 = (bf16[32,3,64]{2,0,1:T(8,128)(2,1)}, bf16[32,3,64]{2,0,1:T(8,128)(2,1)}, u32[]{:S(2)}, u32[]{:S(2)}) collective-permute-start(bf16[32,3,64]{2,0,1:T(8,128)(2,1)} %get-tuple-element.17), channel_id=1, source_target_pairs={{0,1},{1,2},{2,3},{3,4},{4,5},{5,6},{6,7},{7,8},{8,9},{9,10},{10,1... | collective-permute-start | bytes 36872 | tf_op jit(solution)/shard_map/ppermute | solution.py:18
  19.0 4.3 %collective-permute-start.6 = (bf16[32,3,64]{2,0,1:T(8,128)(2,1)}, bf16[32,3,64]{2,0,1:T(8,128)(2,1)}, u32[]{:S(2)}, u32[]{:S(2)}) collective-permute-start(bf16[32,3,64]{2,0,1:T(8,128)(2,1)} %get-tuple-element.13), channel_id=1, source_target_pairs={{0,1},{1,2},{2,3},{3,4},{4,5},{5,6},{6,7},{7,8},{8,9},{9,10},{10,1... | collective-permute-start | bytes 36872 | tf_op jit(solution)/shard_map/ppermute | solution.py:18
  31.9 7.6 %all_gather.6 = f32[32,4,64]{2,0,1:T(8,128)S(1)} all-gather(f32[32,1,64]{2,0,1:T(8,128)S(1)} %convolution_bitcast_fusion.6), channel_id=1, replica_groups=mesh['leaf'=8,'sub'=4] {'sub'}, dimensions={1}, use_global_device_ids=true | all-gather | bytes 40960 | tf_op jit(solution)/shard_map/all_gather | solution.py:167
  39.6 1.9 %reshape.187 = bf16[8,2,64,64]{3,2,1,0:T(8,128)(2,1)} reshape(bf16[16,4096]{1,0:T(8,128)(2,1)} %param.28) | data formatting | bytes 262144 | tf_op jit(solution)/shard_map/reshape | solution.py:165
  42.4 31.6 %all-gather.1 = bf16[8,64,32]{1,2,0:T(8,128)(2,1)S(1)} all-gather(bf16[1,64,32]{1,2,0:T(8,128)(2,1)S(1)} %fusion.20), channel_id=2, replica_groups=mesh['leaf'=8,'sub'=4] {'leaf'}, dimensions={0}, use_global_device_ids=true | all-gather | bytes 36864 | tf_op jit(solution)/shard_map/all_gather | solution.py:169
  93.2 2.6 %reshape.208 = bf16[48,64,64]{2,1,0:T(8,128)(2,1)} reshape(bf16[48,4096]{1,0:T(8,128)(2,1)} %param.23) | data formatting | bytes 786432 | tf_op jit(solution)/shard_map/reshape | solution.py:67
  95.9 2.2 %copy.47 = bf16[96,4096]{0,1:T(8,128)(2,1)} copy(bf16[96,4096]{1,0:T(8,128)(2,1)} %param.22) | data formatting | bytes 1572864 | tf_op args[7]
  98.1 4.1 %copy.48 = bf16[96,64,64]{2,1,0:T(8,128)(2,1)} copy(bf16[96,64,64]{0,2,1:T(8,128)(2,1)} %bitcast.198) | data formatting | bytes 1572864 | tf_op jit(solution)/shard_map/reshape | solution.py:67
  102.2 3.8 %copy.49 = bf16[192,4096]{0,1:T(8,128)(2,1)} copy(bf16[192,4096]{1,0:T(8,128)(2,1)} %param.21) | data formatting | bytes 3145728 | tf_op args[6]
  106.1 5.3 %copy.50 = bf16[192,64,64]{2,1,0:T(8,128)(2,1)} copy(bf16[192,64,64]{0,2,1:T(8,128)(2,1)} %bitcast.196) | data formatting | bytes 3145728 | tf_op jit(solution)/shard_map/reshape | solution.py:67
  112.6 3.7 %collective-permute-start = (bf16[32,2048]{1,0:T(8,128)(2,1)}, bf16[32,2048]{1,0:T(8,128)(2,1)}, u32[]{:S(2)}, u32[]{:S(2)}) collective-permute-start(bf16[32,2048]{1,0:T(8,128)(2,1)} %get-tuple-element.15), channel_id=1, source_target_pairs={{0,1},{1,2},{2,3},{3,4},{4,5},{5,6},{6,7},{7,8},{8,9},{9,10},{10,1... | collective-permute-start | bytes 393224 | tf_op jit(solution)/shard_map/ppermute | solution.py:18
  118.6 2.5 %convolution_multiply_fusion.3 = f32[48,32,64]{2,1,0:T(8,128)} fusion(bf16[48,64,64]{2,1,0:T(8,128)(2,1)} %reshape.208, bf16[48,32,64]{2,1,0:T(8,128)(2,1)} %gather_fusion.1, f32[48]{0:T(128)} %compare_select_fusion.6, pred[48]{0:T(512)(128)(4,1)} %get-tuple-element.5), kind=kOutput, calls=%fused_computation.20 | convolution fusion | flops 12779520 | bytes 983280 | tf_op jit(solution)/shard_map/rsk,skm->rsm/dot_general | solution.py:64
  121.2 1.9 %reduce_sum.105 = f32[32,16,64]{2,0,1:T(8,128)} reduce(f32[32,3,16,64]{3,0,2,1:T(8,128)} %bitcast.199, f32[]{:T(128)} %constant.91.clone.1), dimensions={1}, to_apply=%region_7.8 | reduce | flops 65536 | bytes 524292 | tf_op jit(solution)/shard_map/reduce_sum | solution.py:74
  127.1 3.4 %convolution_multiply_fusion.2 = f32[96,32,64]{2,1,0:T(8,128)} fusion(bf16[96,64,64]{2,1,0:T(8,128)(2,1)} %copy.48, bf16[96,32,64]{2,1,0:T(8,128)(2,1)} %gather_fusion.2, f32[96]{0:T(128)} %compare_select_fusion.5, pred[96]{0:T(512)(128)(4,1)} %get-tuple-element.7), kind=kOutput, calls=%fused_computation.12 | convolution fusion | flops 25559040 | bytes 1966560 | tf_op jit(solution)/shard_map/rsk,skm->rsm/dot_general | solution.py:64
  130.8 2.5 %reduce_sum.106 = f32[32,32,64]{2,0,1:T(8,128)} reduce(f32[32,3,32,64]{3,0,2,1:T(8,128)} %bitcast.197, f32[]{:T(128)} %constant.91.clone.1), dimensions={1}, to_apply=%region_8.9 | reduce | flops 131072 | bytes 1048580 | tf_op jit(solution)/shard_map/reduce_sum | solution.py:74
  134.2 2.0 %gather_fusion.3 = bf16[192,32,64]{2,1,0:T(8,128)(2,1)} fusion(bf16[32,70,64]{2,0,1:T(8,128)(2,1)S(1)} %pad_maximum_fusion, s32[1024]{0:T(1024)S(1)} %pad_clamp_fusion), kind=kCustom, calls=%fused_computation.3 | custom fusion | bytes 1573632 | tf_op jit(solution)/shard_map/jit(_take)/gather | solution.py:63
  136.2 5.2 %convolution_multiply_fusion.1 = f32[192,32,64]{2,1,0:T(8,128)} fusion(bf16[192,64,64]{2,1,0:T(8,128)(2,1)} %copy.50, bf16[192,32,64]{2,1,0:T(8,128)(2,1)} %gather_fusion.3, f32[192]{0:T(256)S(1)} %copy-done.14, pred[192]{0:T(512)(128)(4,1)S(1)} %copy-done.12), kind=kOutput, calls=%fused_computation.5 | convolution fusion | flops 51118080 | bytes 3933120 | tf_op jit(solution)/shard_map/rsk,skm->rsm/dot_general | solution.py:64
  142.5 3.4 %reduce_sum.107 = f32[32,64,64]{2,0,1:T(8,128)} reduce(f32[32,3,64,64]{3,0,2,1:T(8,128)} %bitcast.194, f32[]{:T(128)} %constant.91.clone.1), dimensions={1}, to_apply=%region_9.10 | reduce | flops 262144 | bytes 2097156 | tf_op jit(solution)/shard_map/reduce_sum | solution.py:74
  147.1 2.0 %gather_fusion = bf16[192,32,128]{2,1,0:T(8,128)(2,1)} fusion(bf16[32,96,128]{2,0,1:T(8,128)(2,1)S(1)} %copy_bitcast_fusion.1, s32[1024]{0:T(1024)S(1)} %pad_clamp_fusion.3), kind=kCustom, calls=%fused_computation | custom fusion | bytes 3146496 | tf_op jit(solution)/shard_map/jit(_take)/gather | solution.py:108
  149.1 8.4 %convolution_multiply_fusion = f32[192,32,128]{2,1,0:T(8,128)} fusion(bf16[192,128,128]{2,1,0:T(8,128)(2,1)} %param.17, bf16[192,32,128]{2,1,0:T(8,128)(2,1)} %gather_fusion, f32[192]{0:T(256)S(1)} %copy-done.13, pred[192]{0:T(512)(128)(4,1)S(1)} %copy-done.11), kind=kOutput, calls=%fused_computation.4 | convolution fusion | flops 202899456 | bytes 11011008 | tf_op jit(solution)/shard_map/bij,rbj->rbi/dot_general | solution.py:109
  157.5 3.4 %reduce_sum.98 = f32[32,64,128]{2,0,1:T(8,128)} reduce(f32[32,3,64,128]{3,0,2,1:T(8,128)} %bitcast.195, f32[]{:T(128)} %constant.91.clone.1), dimensions={1}, to_apply=%region_0.1 | reduce | flops 524288 | bytes 4194308 | tf_op jit(solution)/shard_map/reduce_sum | solution.py:118
  161.8 3.3 %fusion.7 = f32[64,4,8,128]{3,2,1,0:T(8,128)} fusion(f32[32,64,128]{2,0,1:T(8,128)} %reduce_sum.98, bf16[64,64,128]{2,1,0:T(8,128)(2,1)S(1)} %copy-done, f32[32,64,64]{2,0,1:T(8,128)S(1)} %copy-done.3, bf16[32,64,64]{2,0,1:T(8,128)(2,1)} %bitcast.200, bf16[64,64,64]{2,1,0:T(8,128)(2,1)S(1)} %reshape.190), kind=kOutput, calls=%fused_computation.15 | convolution fusion | flops 50855936 | bytes 4456448 | tf_op jit(solution)/shard_map/rlk,lkp->rlp/dot_general | solution.py:189
  165.1 2.3 %copy.67 = f32[64,4,8,128]{3,2,0,1:T(8,128)} copy(f32[64,4,8,128]{3,2,1,0:T(8,128)} %fusion.7) | data formatting | bytes 2097152 | tf_op jit(solution)/shard_map/reshape | solution.py:195
  (111 shorter events, 50.6 us)
Async XLA Ops:
  0.0 3.0 %copy-start = (bf16[64,64,128]{2,1,0:T(8,128)(2,1)S(1)}, bf16[64,64,128]{2,1,0:T(8,128)(2,1)}, u32[]{:S(2)}) copy-start(bf16[64,64,128]{2,1,0:T(8,128)(2,1)} %param.16) | copy-start | bytes 3145732
  0.0 2.5 %slice-start.1 = ((bf16[127,4096]{1,0:T(8,128)(2,1)}), bf16[32,4096]{1,0:T(8,128)(2,1)S(1)}, s32[]{:S(2)}) async-start(bf16[127,4096]{1,0:T(8,128)(2,1)} %param.20), calls=%async_computation.1 | async-start | bytes 524288 | tf_op jit(solution)/shard_map/slice | solution.py:124
  3.1 2.3 %copy-start.1 = (bf16[32,64,64]{2,1,0:T(8,128)(2,1)}, bf16[32,64,64]{2,1,0:T(8,128)(2,1)S(1)}, u32[]{:S(2)}) copy-start(bf16[32,64,64]{2,1,0:T(8,128)(2,1)S(1)} %reshape.192) | copy-start | bytes 786436
  5.4 23.9 %slice-start.2 = ((bf16[127,4096]{1,0:T(8,128)(2,1)}), bf16[8,4096]{1,0:T(8,128)(2,1)S(1)}, s32[]{:S(2)}) async-start(bf16[127,4096]{1,0:T(8,128)(2,1)} %param.20), calls=%async_computation.2 | async-start | bytes 131072 | tf_op jit(solution)/shard_map/slice | solution.py:124
  5.4 24.1 %slice-start.3 = ((bf16[127,4096]{1,0:T(8,128)(2,1)}), bf16[4,4096]{1,0:T(4,128)(2,1)S(1)}, s32[]{:S(2)}) async-start(bf16[127,4096]{1,0:T(8,128)(2,1)} %param.20), calls=%async_computation.3 | async-start | bytes 65536 | tf_op jit(solution)/shard_map/slice | solution.py:124
  6.9 21.5 %copy-start.7 = (bf16[32,16,64]{2,0,1:T(8,128)(2,1)S(1)}, bf16[32,16,64]{2,0,1:T(8,128)(2,1)}, u32[]{:S(2)}) copy-start(bf16[32,16,64]{2,0,1:T(8,128)(2,1)} %copy-done.6) | copy-start | bytes 196612
  6.9 104.4 %collective-permute-start.2 = (bf16[32,3,64]{2,0,1:T(8,128)(2,1)}, bf16[32,3,64]{2,0,1:T(8,128)(2,1)}, u32[]{:S(2)}, u32[]{:S(2)}) collective-permute-start(bf16[32,3,64]{2,0,1:T(8,128)(2,1)} %get-tuple-element.19), channel_id=1, source_target_pairs={{0,1},{1,2},{2,3},{3,4},{4,5},{5,6},{6,7},{7,8},{8,9},{9,10},{10,1... | collective-permute-start | bytes 36872 | tf_op jit(solution)/shard_map/ppermute | solution.py:18
  10.0 102.6 %collective-permute-start.3 = (bf16[32,3,64]{2,0,1:T(8,128)(2,1)}, bf16[32,3,64]{2,0,1:T(8,128)(2,1)}, u32[]{:S(2)}, u32[]{:S(2)}) collective-permute-start(bf16[32,3,64]{2,0,1:T(8,128)(2,1)} %get-tuple-element.20), channel_id=1, source_target_pairs={{1,0},{2,1},{3,2},{4,3},{5,4},{6,5},{7,6},{8,7},{9,8},{10,9},{11,1... | collective-permute-start | bytes 36872 | tf_op jit(solution)/shard_map/ppermute | solution.py:21
  11.9 111.2 %collective-permute-start.4 = (bf16[32,3,64]{2,0,1:T(8,128)(2,1)}, bf16[32,3,64]{2,0,1:T(8,128)(2,1)}, u32[]{:S(2)}, u32[]{:S(2)}) collective-permute-start(bf16[32,3,64]{2,0,1:T(8,128)(2,1)} %get-tuple-element.17), channel_id=1, source_target_pairs={{0,1},{1,2},{2,3},{3,4},{4,5},{5,6},{6,7},{7,8},{8,9},{9,10},{10,1... | collective-permute-start | bytes 36872 | tf_op jit(solution)/shard_map/ppermute | solution.py:18
  17.1 107.5 %collective-permute-start.5 = (bf16[32,3,64]{2,0,1:T(8,128)(2,1)}, bf16[32,3,64]{2,0,1:T(8,128)(2,1)}, u32[]{:S(2)}, u32[]{:S(2)}) collective-permute-start(bf16[32,3,64]{2,0,1:T(8,128)(2,1)} %get-tuple-element.18), channel_id=1, source_target_pairs={{1,0},{2,1},{3,2},{4,3},{5,4},{6,5},{7,6},{8,7},{9,8},{10,9},{11,1... | collective-permute-start | bytes 36872 | tf_op jit(solution)/shard_map/ppermute | solution.py:21
  19.0 114.3 %collective-permute-start.6 = (bf16[32,3,64]{2,0,1:T(8,128)(2,1)}, bf16[32,3,64]{2,0,1:T(8,128)(2,1)}, u32[]{:S(2)}, u32[]{:S(2)}) collective-permute-start(bf16[32,3,64]{2,0,1:T(8,128)(2,1)} %get-tuple-element.13), channel_id=1, source_target_pairs={{0,1},{1,2},{2,3},{3,4},{4,5},{5,6},{6,7},{7,8},{8,9},{9,10},{10,1... | collective-permute-start | bytes 36872 | tf_op jit(solution)/shard_map/ppermute | solution.py:18
  106.1 5.3 %copy-start.10 = (bf16[32,3,64]{2,0,1:T(8,128)(2,1)S(1)}, bf16[32,3,64]{2,0,1:T(8,128)(2,1)}, u32[]{:S(2)}) copy-start(bf16[32,3,64]{2,0,1:T(8,128)(2,1)} %get-tuple-element.14) | copy-start | bytes 36868
  111.3 21.9 %collective-permute-start.7 = (bf16[32,3,64]{2,0,1:T(8,128)(2,1)S(1)}, bf16[32,3,64]{2,0,1:T(8,128)(2,1)}, u32[]{:S(2)}, u32[]{:S(2)}) collective-permute-start(bf16[32,3,64]{2,0,1:T(8,128)(2,1)S(1)} %copy-done.10), channel_id=1, source_target_pairs={{1,0},{2,1},{3,2},{4,3},{5,4},{6,5},{7,6},{8,7},{9,8},{10,9},{11,1... | collective-permute-start | bytes 36872 | tf_op jit(solution)/shard_map/ppermute | solution.py:21
  112.6 33.3 %collective-permute-start = (bf16[32,2048]{1,0:T(8,128)(2,1)}, bf16[32,2048]{1,0:T(8,128)(2,1)}, u32[]{:S(2)}, u32[]{:S(2)}) collective-permute-start(bf16[32,2048]{1,0:T(8,128)(2,1)} %get-tuple-element.15), channel_id=1, source_target_pairs={{0,1},{1,2},{2,3},{3,4},{4,5},{5,6},{6,7},{7,8},{8,9},{9,10},{10,1... | collective-permute-start | bytes 393224 | tf_op jit(solution)/shard_map/ppermute | solution.py:18
  123.1 22.9 %collective-permute-start.1 = (bf16[32,2048]{1,0:T(8,128)(2,1)}, bf16[32,2048]{1,0:T(8,128)(2,1)}, u32[]{:S(2)}, u32[]{:S(2)}) collective-permute-start(bf16[32,2048]{1,0:T(8,128)(2,1)} %get-tuple-element.16), channel_id=1, source_target_pairs={{1,0},{2,1},{3,2},{4,3},{5,4},{6,5},{7,6},{8,7},{9,8},{10,9},{11,1... | collective-permute-start | bytes 393224 | tf_op jit(solution)/shard_map/ppermute | solution.py:21
  127.1 3.5 %copy-start.8 = (f32[32,16,64]{2,0,1:T(8,128)S(1)}, f32[32,16,64]{2,0,1:T(8,128)}, u32[]{:S(2)}) copy-start(f32[32,16,64]{2,0,1:T(8,128)} %reduce_sum.105) | copy-start | bytes 393220
  134.2 2.0 %copy-start.12 = (pred[192]{0:T(512)(128)(4,1)S(1)}, pred[192]{0:T(512)(128)(4,1)}, u32[]{:S(2)}) copy-start(pred[192]{0:T(512)(128)(4,1)} %get-tuple-element.9) | copy-start | bytes 580
  134.2 2.0 %copy-start.14 = (f32[192]{0:T(256)S(1)}, f32[192]{0:T(256)}, u32[]{:S(2)}) copy-start(f32[192]{0:T(256)} %compare_select_fusion.4) | copy-start | bytes 2308
  136.2 5.2 %copy-start.2 = (bf16[32,64,64]{2,1,0:T(8,128)(2,1)S(1)}, bf16[32,64,64]{2,1,0:T(8,128)(2,1)}, u32[]{:S(2)}) copy-start(bf16[32,64,64]{2,1,0:T(8,128)(2,1)} %copy-done.1) | copy-start | bytes 786436
  136.2 5.2 %copy-start.5 = (f32[32,32,64]{2,0,1:T(8,128)S(1)}, f32[32,32,64]{2,0,1:T(8,128)}, u32[]{:S(2)}) copy-start(f32[32,32,64]{2,0,1:T(8,128)} %reduce_sum.106) | copy-start | bytes 786436
  142.5 3.5 %copy-start.4 = (bf16[32,8192]{1,0:T(8,128)(2,1)S(1)}, bf16[32,8192]{1,0:T(8,128)(2,1)}, u32[]{:S(2)}) copy-start(bf16[32,8192]{1,0:T(8,128)(2,1)} %param.15) | copy-start | bytes 1572868
  147.1 2.0 %copy-start.11 = (pred[192]{0:T(512)(128)(4,1)S(1)}, pred[192]{0:T(512)(128)(4,1)}, u32[]{:S(2)}) copy-start(pred[192]{0:T(512)(128)(4,1)} %get-tuple-element.11) | copy-start | bytes 580
  157.5 3.4 %copy-start.9 = (bf16[32,32,64]{2,0,1:T(8,128)(2,1)S(1)}, bf16[32,32,64]{2,0,1:T(8,128)(2,1)}, u32[]{:S(2)}) copy-start(bf16[32,32,64]{2,0,1:T(8,128)(2,1)} %fusion.12) | copy-start | bytes 393220
  157.5 4.3 %copy-start.3 = (f32[32,64,64]{2,0,1:T(8,128)S(1)}, f32[32,64,64]{2,0,1:T(8,128)}, u32[]{:S(2)}) copy-start(f32[32,64,64]{2,0,1:T(8,128)} %reduce_sum.107) | copy-start | bytes 1572868
  (3 other events, 4.0 us)
where the time goes:
time: 170 us; the launch traced here: 167 us
  local copies, waits for them, and re-layouts  47.7 us (28%)
  blocking collectives  39.2 us (23%)
  matrix products  32.7 us (19%)
  other arithmetic  25.1 us (15%)
  starting transfers between devices  21.5 us (13%)
    all_gather x1, blocking collectives, local(): lax.all_gather(kept_levels[-1][:, 0], 'leaf', axis=1, tiled=True)  31.6 us
    ppermute x4, starting transfers between devices, with_halo(): lax.ppermute(lax.slice_in_dim(block, block.shape[dim] - width, None, axis...  16.2 us
    reshape x3, local copies, waits for them, and re-layouts, couple_level(): matrices.reshape(slot_count, rank_size, rank_size)  12 us
    dot_general x3, matrix products, couple_level(): jnp.einsum('rsk,skm->rsm', picked, matrices.reshape(slot_count, rank_size...  11.1 us
    dot_general x1, matrix products, local(): jnp.einsum('bij,rbj->rbi', near_blocks, picked, preferred_element_type=jn...  8.36 us
    reduce_sum x3, other arithmetic, couple_level(): products.reshape(products.shape[0], slot_count // node_count, node_count,...  7.83 us
    unnamed x33, local copies, waits for them, and re-layouts  7.72 us
    all_gather x1, blocking collectives, local(): group_terms = lax.all_gather(top_terms, 'sub', axis=1, tiled=True)  7.63 us
  transfers between devices with their start and end apart: 8, of which 0 were waited for; matrix products, arithmetic and copies ran while one was open for 46% of the time, Pallas kernels for 0%

commit v1 on v0

v1 whole, which is shorter than its diff:
```python
import functools

import jax
import jax.numpy as jnp
from jax import lax
from jax.experimental import pallas as pl
from jax.experimental.pallas import tpu as pltpu
from jax.sharding import PartitionSpec as P

REACH = 16
COUPLED = 3
HALO = 3
CHUNKS = 4
MESH = pl.DeviceIdType.MESH
BF = jnp.bfloat16
F32 = jnp.float32


def dot_nn(a, b):
    return lax.dot_general(a, b, (((1,), (0,)), ((), ())), preferred_element_type=F32)


def dot_nt(a, b):
    return lax.dot_general(a, b, (((1,), (1,)), ((), ())), preferred_element_type=F32)


def spread(rank):
    row = lax.broadcasted_iota(jnp.int32, (2 * rank, 2 * rank), 0)
    col = lax.broadcasted_iota(jnp.int32, (2 * rank, 2 * rank), 1)
    inner = row % rank
    place = (row // rank) * rank + (inner % 2) * (rank // 2) + inner // 2
    return jnp.where(place == col, 1.0, 0.0).astype(BF)


def kernel(
    dims,
    idx,
    sources,
    basis,
    near,
    transfer,
    first,
    second,
    third,
    fold,
    top,
    out,
    xs,
    xl,
    vb,
    vn,
    vt,
    v1,
    v2,
    v3,
    vf,
    vtop,
    ft,
    f1,
    f2,
    f3,
    ff,
    ftop,
    wt,
    cp0,
    cp1,
    cp2,
    chi,
    g0,
    g1,
    g2,
    dn,
    terms,
    tc,
    load_sem,
    near_sem,
    halo_send,
    halo_recv,
    coef_send,
    coef_recv,
    sub_send,
    sub_recv,
    leaf_send,
    leaf_recv,
):
    groups, members, leaves, columns, rank, points = dims
    depth = leaves.bit_length() - 1
    lf = lax.axis_index("leaf")
    sb = lax.axis_index("sub")
    me = lf * members + sb
    count = groups * members
    right = lax.rem(me + 1, count)
    left = lax.rem(me + count - 1, count)
    right_id = (right // members, lax.rem(right, members))
    left_id = (left // members, lax.rem(left, members))
    half = rank // 2
    wide = REACH * points
    own = leaves * points

    loads = []
    pairs = (
        (transfer, vt),
        (sources, xs.at[:, pl.ds(wide, own)]),
        (basis, vb),
        (fold, vf),
        (top, vtop),
        (first, v1),
        (second, v2),
        (third, v3),
    )
    for i, (src, dst) in enumerate(pairs):
        copy = pltpu.make_async_copy(src, dst, load_sem.at[i])
        copy.start()
        loads.append(copy)
    part = leaves // CHUNKS
    near_loads = []
    for i in range(CHUNKS):
        copy = pltpu.make_async_copy(
            near.at[:, pl.ds(i * part, part)], vn.at[:, pl.ds(i * part, part)], near_sem.at[i]
        )
        copy.start()
        near_loads.append(copy)

    sub_ids = [(lf, lax.rem(sb + k, members)) for k in range(1, members)]
    leaf_ids = [(lax.rem(lf + k, groups), sb) for k in range(1, groups)]
    everyone = [left_id, right_id] + sub_ids + leaf_ids
    barrier = pltpu.get_barrier_semaphore()
    for target in everyone:
        pl.semaphore_signal(barrier, inc=1, device_id=target, device_id_type=MESH)

    perm = spread(rank)
    small = perm[:rank, :rank]

    def relay(src, dst):
        rows = src.shape[0]
        step = 8

        def body(q, carry):
            vals = []
            for u in range(step):
                p = q * step + u
                block = src[:, pl.ds(pl.multiple_of(p * 2 * rank, 2 * rank), 2 * rank)]
                vals.append(dot_nn(block, perm))
            for u in range(step):
                dst[pl.ds(q * step + u, rows, stride=half), :] = vals[u]
            return carry

        lax.fori_loop(0, half // step, body, 0)

    def matrix(ref, s):
        m = ref[pl.ds(pl.multiple_of(s * half, half), half), :].astype(BF)
        return jnp.concatenate([m[:, :rank], m[:, rank:]], axis=0)

    def blocks(n, width, compute, store):
        width = min(width, n)

        def body(q, carry):
            vals = [compute(q * width + u) for u in range(width)]
            for u in range(width):
                store(q * width + u, vals[u])
            return carry

        if n == width:
            body(0, 0)
        else:
            lax.fori_loop(0, n // width, body, 0)

    loads[0].wait()
    relay(vt, ft)

    def put_wt(s, value):
        wt[s] = value

    for start in range(2 * leaves - 1 - (2 * leaves - 1) % 8, 2 * leaves - 1):
        wt[start] = matrix(ft, start)
    blocks((2 * leaves - 1) // 8 * 8, 8, functools.partial(matrix, ft), put_wt)

    pl.semaphore_wait(barrier, len(everyone))
    halo = [
        pltpu.make_async_remote_copy(
            src_ref=sources.at[:, pl.ds(own - wide, wide)],
            dst_ref=xs.at[:, pl.ds(0, wide)],
            send_sem=halo_send.at[0],
            recv_sem=halo_recv.at[0],
            device_id=right_id,
            device_id_type=MESH,
        ),
        pltpu.make_async_remote_copy(
            src_ref=sources.at[:, pl.ds(0, wide)],
            dst_ref=xs.at[:, pl.ds(wide + own, wide)],
            send_sem=halo_send.at[1],
            recv_sem=halo_recv.at[1],
            device_id=left_id,
            device_id_type=MESH,
        ),
    ]
    for copy in halo:
        copy.start()

    every = leaves + 2 * REACH
    xl[every] = jnp.zeros((columns, points), BF)
    coefs = (cp0, cp1, cp2)
    for j, ref in enumerate(coefs):
        ref[(leaves >> j) + 2 * HALO] = jnp.zeros((columns, rank), BF)

    loads[1].wait()
    loads[2].wait()

    def leaf_body(q, carry):
        vals = []
        for u in range(8):
            leaf = q * 8 + u
            x = xs[:, pl.ds(pl.multiple_of(wide + leaf * points, points), points)]
            vals.append(dot_nt(x, vb[leaf]).astype(BF))
        mixed = dot_nn(jnp.concatenate(vals, axis=0), small).astype(BF)
        for u in range(8):
            cp0[HALO + q * 8 + u] = mixed[u * columns : (u + 1) * columns]
        return carry

    lax.fori_loop(0, leaves // 8, leaf_body, 0)

    high_start = {}
    position = 0
    for j in range(COUPLED, depth + 1):
        high_start[j] = position
        position += leaves >> j

    def place(j):
        return (coefs[j], HALO) if j < COUPLED else (chi, high_start[j])

    for j in range(depth):
        src, src_at = place(j)
        dst, dst_at = place(j + 1)
        row = 2 * leaves - 2 * (leaves >> j)

        def up(n, src=src, src_at=src_at, row=row):
            a = dot_nn(src[src_at + 2 * n], wt[row + 2 * n])
            b = dot_nn(src[src_at + 2 * n + 1], wt[row + 2 * n + 1])
            return (a + b).astype(BF)

        def put(n, value, dst=dst, dst_at=dst_at):
            dst[dst_at + n] = value

        blocks(leaves >> (j + 1), 8, up, put)

    root = 2 * leaves - 2
    terms[sb] = dot_nn(chi[high_start[depth]], wt[root])
    sub_copies = [
        pltpu.make_async_remote_copy(
            src_ref=terms.at[sb],
            dst_ref=terms.at[sb],
            send_sem=sub_send.at[k],
            recv_sem=sub_recv.at[k],
            device_id=target,
            device_id_type=MESH,
        )
        for k, target in enumerate(sub_ids)
    ]
    for copy in sub_copies:
        copy.start()
    coef_copies = []
    for j, ref in enumerate(coefs):
        n = leaves >> j
        for side, (src_at, dst_at, target) in enumerate(
            ((n, 0, right_id), (HALO, n + HALO, left_id))
        ):
            copy = pltpu.make_async_remote_copy(
                src_ref=ref.at[pl.ds(src_at, HALO)],
                dst_ref=ref.at[pl.ds(dst_at, HALO)],
                send_sem=coef_send.at[2 * j + side],
                recv_sem=coef_recv.at[2 * j + side],
                device_id=target,
                device_id_type=MESH,
            )
            copy.start()
            coef_copies.append(copy)

    loads[3].wait()
    relay(vf, ff)
    loads[4].wait()
    relay(vtop, ftop)

    for copy in sub_copies:
        copy.wait()
    fold_row = lf * (members - 2)
    current = [(terms[2 * n] + terms[2 * n + 1]).astype(BF) for n in range(members // 2)]
    offset = 0
    while len(current) > 1:
        products = [
            dot_nn(c, matrix(ff, fold_row + offset + n)) for n, c in enumerate(current)
        ]
        offset += len(current)
        current = [
            (products[2 * n] + products[2 * n + 1]).astype(BF)
            for n in range(len(products) // 2)
        ]
    tc[lf] = current[0]
    leaf_copies = [
        pltpu.make_async_remote_copy(
            src_ref=tc.at[lf],
            dst_ref=tc.at[lf],
            send_sem=leaf_send.at[k],
            recv_sem=leaf_recv.at[k],
            device_id=target,
            device_id_type=MESH,
        )
        for k, target in enumerate(leaf_ids)
    ]
    for copy in leaf_copies:
        copy.start()

    loads[5].wait()
    relay(v1, f1)
    loads[6].wait()
    relay(v2, f2)
    loads[7].wait()
    relay(v3, f3)
    for copy in coef_copies:
        copy.wait()
    base = 3 * leaves
    for j, (mats, field) in enumerate(((f1, g0), (f2, g1), (f3, g2))):
        n = leaves >> j
        ref = coefs[j]

        def couple(i, n=n, ref=ref, mats=mats, base=base):
            total = None
            for t in range(3):
                s = t * n + i
                value = dot_nn(ref[idx[base + s]], matrix(mats, s))
                total = value if total is None else total + value
            return total

        def put_field(i, value, field=field):
            field[i] = value

        blocks(n, 8, couple, put_field)
        base += 3 * n

    for copy in halo:
        copy.wait()
    for copy in near_loads:
        copy.wait()

    def load_leaf(leaf):
        return xs[:, pl.ds(pl.multiple_of(leaf * points, points), points)]

    def put_leaf(leaf, value):
        xl[leaf] = value

    blocks(every, 8, load_leaf, put_leaf)

    def near_leaf(leaf):
        total = None
        for t in range(3):
            value = dot_nt(xl[idx[t * leaves + leaf]], vn[t, leaf])
            total = value if total is None else total + value
        return total

    def put_near(leaf, value):
        out[:, pl.ds(pl.multiple_of(leaf * points, points), points)] = value

    blocks(leaves, 8, near_leaf, put_near)

    for copy in leaf_copies:
        copy.wait()
    down = jnp.zeros((columns, rank), F32)
    for t in range(groups):
        far = jnp.where(jnp.abs(lf - t) >= 2, 1.0, 0.0).astype(F32)
        down = down + far * dot_nn(tc[t], matrix(ftop, t))
    nodes = 2
    while nodes <= members // 2:
        row = fold_row + members - 2 * nodes + sb * nodes // members
        down = dot_nt(down.astype(BF), matrix(ff, row))
        nodes *= 2
    down = dot_nt(down.astype(BF), wt[root])
    down_start = {depth: 0}
    position = 1
    for j in reversed(range(depth)):
        down_start[j] = position
        position += leaves >> j
    dn[0] = down.astype(BF)
    fields = (g0, g1, g2)
    for j in reversed(range(depth)):
        row = 2 * leaves - 2 * (leaves >> j)
        src_at, dst_at = down_start[j + 1], down_start[j]

        def descend(c, row=row, src_at=src_at, j=j):
            value = dot_nt(dn[src_at + c // 2], wt[row + c])
            if j < COUPLED:
                value = value + fields[j][c]
            return value.astype(BF)

        def put_down(c, value, dst_at=dst_at):
            dn[dst_at + c] = value

        blocks(leaves >> j, 8, descend, put_down)

    def final_body(q, carry):
        rows = jnp.concatenate([dn[down_start[0] + q * 8 + u] for u in range(8)], axis=0)
        natural = dot_nt(rows, small).astype(BF)
        for u in range(8):
            leaf = q * 8 + u
            at = pl.ds(pl.multiple_of(leaf * points, points), points)
            out[:, at] = out[:, at] + dot_nn(
                natural[u * columns : (u + 1) * columns], vb[leaf]
            )
        return carry

    lax.fori_loop(0, leaves // 8, final_body, 0)


def local(
    sources,
    leaf_basis,
    near_blocks,
    near_index,
    near_count,
    transfer,
    couple_first,
    couple_second,
    couple_third,
    index_first,
    index_second,
    index_third,
    couple_count,
    fold_transfer,
    top_couple,
):
    columns = sources.shape[0]
    leaves, rank, points = leaf_basis.shape
    groups = lax.axis_size("leaf")
    members = lax.axis_size("sub")
    device = lax.axis_index(("leaf", "sub"))

    def slots(index, live, first_node, dead):
        n = index.shape[0]
        return jnp.where(lax.iota(jnp.int32, n) < live, index[:, 1] - first_node, dead)

    lists = [slots(near_index, near_count[0], device * leaves - REACH, leaves + 2 * REACH)]
    for j, index in enumerate((index_first, index_second, index_third)):
        n = leaves >> j
        lists.append(slots(index, couple_count[0, j], device * n - HALO, n + 2 * HALO))
    idx = jnp.concatenate(lists)

    near = near_blocks.reshape(3, leaves, points, points)
    top = top_couple.reshape(groups, rank * rank)
    trans = transfer.shape[0]
    half = rank // 2

    def flat(n):
        return pltpu.VMEM((n * half, 2 * rank), F32)

    scratch = [
        pltpu.VMEM((columns, (leaves + 2 * REACH) * points), BF),
        pltpu.VMEM((leaves + 2 * REACH + 1, columns, points), BF),
        pltpu.VMEM(leaf_basis.shape, BF),
        pltpu.VMEM(near.shape, BF),
        pltpu.VMEM(transfer.shape, BF),
        pltpu.VMEM(couple_first.shape, BF),
        pltpu.VMEM(couple_second.shape, BF),
        pltpu.VMEM(couple_third.shape, BF),
        pltpu.VMEM(fold_transfer.shape, BF),
        pltpu.VMEM(top.shape, BF),
        flat(trans),
        flat(couple_first.shape[0]),
        flat(couple_second.shape[0]),
        flat(couple_third.shape[0]),
        flat(fold_transfer.shape[0]),
        flat(groups),
        pltpu.VMEM((trans, rank, rank), BF),
    ]
    for j in range(COUPLED):
        scratch.append(pltpu.VMEM(((leaves >> j) + 2 * HALO + 1, columns, rank), BF))
    scratch.append(pltpu.VMEM(((leaves >> (COUPLED - 1)) - 1, columns, rank), BF))
    for j in range(COUPLED):
        scratch.append(pltpu.VMEM((leaves >> j, columns, rank), F32))
    scratch.append(pltpu.VMEM((2 * leaves - 1, columns, rank), BF))
    scratch.append(pltpu.VMEM((members, columns, rank), F32))
    scratch.append(pltpu.VMEM((groups, columns, rank), BF))
    for n in (8, CHUNKS, 2, 2, 6, 6, members - 1, members - 1, groups - 1, groups - 1):
        scratch.append(pltpu.SemaphoreType.DMA((n,)))

    anywhere = pl.BlockSpec(memory_space=pl.ANY)
    dims = (groups, members, leaves, columns, rank, points)
    return pl.pallas_call(
        functools.partial(kernel, dims),
        out_shape=jax.ShapeDtypeStruct((columns, leaves * points), F32),
        in_specs=[pl.BlockSpec(memory_space=pltpu.SMEM)] + [anywhere] * 9,
        out_specs=pl.BlockSpec(memory_space=pltpu.VMEM),
        scratch_shapes=scratch,
        compiler_params=pltpu.CompilerParams(
            collective_id=0, has_side_effects=True, vmem_limit_bytes=56 * 1024 * 1024
        ),
        cost_estimate=pl.CostEstimate(
            flops=600_000_000, bytes_accessed=13_000_000, transcendentals=0
        ),
        name="operator",
    )(
        idx,
        sources,
        leaf_basis,
        near,
        transfer,
        couple_first,
        couple_second,
        couple_third,
        fold_transfer,
        top,
    )


def solution(mesh):
    both = ("leaf", "sub")
    return jax.shard_map(
        local,
        mesh=mesh,
        in_specs=(
            P(None, both),
            P(both, None, None),
            P(both, None, None),
            P(both, None),
            P(both),
            P(both, None),
            P(both, None),
            P(both, None),
            P(both, None),
            P(both, None),
            P(both, None),
            P(both, None),
            P(both, None),
            P(),
            P("leaf", None, None),
        ),
        out_specs=P(None, both),
        check_vma=False,
    )
```

time: 170 us -> 46.1 us (0.27); the launches traced: 167 us -> 45.8 us
  local copies, waits for them, and re-layouts: 47.7 us -> 3.68 us
  blocking collectives: 39.2 us -> 0 us
  Pallas kernels: 0 us -> 36.1 us
  matrix products: 32.7 us -> 0 us
  starting transfers between devices: 21.5 us -> 0 us
  other arithmetic: 25.1 us -> 5.32 us
    all_gather x2 -> x0, blocking collectives: 39.2 us -> none  [the longest x1 31.6 us: local(): lax.all_gather(kept_levels[-1][:, 0], 'leaf', axis=1, tiled=True)]
    pallas_call x0 -> x1, Pallas kernels: none -> 36.1 us  [local(): pl.pallas_call(functools.partial(kernel, dims), out_shape=jax.ShapeDtypeS...]
    dot_general x22 -> x0, matrix products: 32.7 us -> none  [the longest x3 11.1 us: couple_level(): jnp.einsum('rsk,skm->rsm', picked, matrices.reshape(slot_count, rank_size...]
    ppermute x8 -> x0, starting transfers between devices: 21.5 us -> none  [the longest x4 16.2 us: with_halo(): lax.ppermute(lax.slice_in_dim(block, block.shape[dim] - width, None, axis...]
    reshape x12 -> x0, local copies, waits for them, and re-layouts: 20.1 us -> none  [the longest x3 12 us: couple_level(): matrices.reshape(slot_count, rank_size, rank_size)]
    reduce_sum x5 -> x0, other arithmetic: 11.2 us -> none  [the longest x3 7.83 us: couple_level(): products.reshape(products.shape[0], slot_count // node_count, node_count,...]
    slice x16 -> x1, local copies, waits for them, and re-layouts: 9.56 us -> 1.41 us  [local(): couple_count[0, j]]
    gather x4 -> x0, local copies, waits for them, and re-layouts: 7.16 us -> none  [the longest x3 5.17 us: couple_level(): picked = jnp.take(padded, indices[:, 1] - first_node, axis=1)]
  transfers between devices with their start and end apart: 8 -> 0, of which waited for: 0 -> 0; matrix products, arithmetic and copies ran while one was open for 46% -> 0% of each run, Pallas kernels for 0% -> 0%
where the time goes in v1:
time: 46.1 us; the launch traced here: 45.8 us
  Pallas kernels  36.1 us (78%)
  other arithmetic  5.32 us (12%)
  local copies, waits for them, and re-layouts  3.68 us (8%)
  between operations  0.67 us (1%)
    pallas_call x1, Pallas kernels, local(): pl.pallas_call(functools.partial(kernel, dims), out_shape=jax.ShapeDtypeS...  36.1 us
    select_n x3, other arithmetic, slots(): jnp.where(lax.iota(jnp.int32, n) < live, index[:, 1] - first_node, dead)  3.28 us
    unnamed x1, local copies, waits for them, and re-layouts  2.26 us
    slice x1, local copies, waits for them, and re-layouts, local(): couple_count[0, j]  1.41 us
    sub x2, other arithmetic, slots(): index[:, 1] - first_node  1.37 us

profile of v1, /device:TPU:0, one launch (start us, length us, event | category | flops | bytes accessed | tf_op | source)
XLA Modules:
  0.0 45.8 jit_solution(16431266882076957521)
XLA Ops:
  0.7 0.7 %slice_subtract_fusion.1 = s32[192,1]{0,1:T(1,128)S(1)} fusion(s32[192,2]{0,1:T(2,128)} %param.18, s32[]{:T(128)S(6)} %sub.48), kind=kLoop, calls=%fused_computation.6 | loop fusion | flops 192 | bytes 1540 | tf_op jit(solution)/shard_map/sub | solution.py:437
  1.3 0.7 %slice_subtract_fusion = s32[192,1]{0,1:T(1,128)S(1)} fusion(s32[192,2]{0,1:T(2,128)} %param.24, s32[]{:T(128)S(6)} %sub.52), kind=kLoop, calls=%fused_computation.5 | loop fusion | flops 192 | bytes 1540 | tf_op jit(solution)/shard_map/sub | solution.py:437
  2.0 1.4 %fusion = (s32[1,1]{1,0:T(1,128)}, s32[1,1]{1,0:T(1,128)}, s32[1,1]{1,0:T(1,128)}) fusion(s32[1,3]{1,0:T(1,128)} %param.27), kind=kLoop, calls=%fused_computation.7 | loop fusion | bytes 24 | tf_op jit(solution)/shard_map/slice | solution.py:442
  3.4 0.6 %compare_select_fusion.2 = (s32[192]{0:T(256)S(1)}, s32[192]{0:T(256)S(1)}) fusion(s32[192]{0:T(256)S(1)} %bitcast.16, s32[]{:T(128)} %bitcast.2, s32[192]{0:T(256)S(1)} %bitcast.15, s32[]{:T(128)} %bitcast.12), kind=kLoop, calls=%fused_computation.3 | loop fusion | flops 768 | bytes 3080 | tf_op jit(solution)/shard_map/jit(_where)/select_n | solution.py:437
  4.1 1.3 %compare_select_fusion = s32[48]{0:T(128)S(1)} fusion(s32[48,2]{0,1:T(2,128)} %param.26, s32[]{:T(128)S(6)} %sub.60, s32[]{:T(128)} %bitcast.6), kind=kLoop, calls=%fused_computation.1 | loop fusion | flops 144 | bytes 392 | tf_op jit(solution)/shard_map/jit(_where)/select_n | solution.py:437
  5.4 1.3 %compare_select_fusion.1 = s32[96]{0:T(128)S(1)} fusion(s32[96,2]{0,1:T(2,128)} %param.25, s32[]{:T(128)S(6)} %sub.56, s32[]{:T(128)} %bitcast.4), kind=kLoop, calls=%fused_computation.2 | loop fusion | flops 288 | bytes 776 | tf_op jit(solution)/shard_map/jit(_where)/select_n | solution.py:437
  6.7 0.7 %pad_add_fusion.idx = s32[528]{0:T(1024)} fusion(s32[48]{0:T(128)S(1)} %compare_select_fusion, s32[96]{0:T(128)S(1)} %compare_select_fusion.1, s32[192]{0:T(256)S(1)} %get-tuple-element.8, s32[192]{0:T(256)S(1)} %get-tuple-element.9), kind=kLoop, calls=%fused_computation | loop fusion | flops 1584 | bytes 4224 | tf_op jit(solution)/shard_map/concatenate | solution.py:443
  7.4 36.1 %operator.1 = f32[32,8192]{1,0:T(8,128)} custom-call(s32[528]{0:T(1024)} %pad_add_fusion.idx, bf16[32,8192]{1,0:T(8,128)(2,1)} %sources.1, bf16[64,64,128]{2,1,0:T(8,128)(2,1)} %basis.1, bf16[3,64,128,128]{3,2,1,0:T(8,128)(2,1)} %bitcast.13, bf16[127,4096]{1,0:T(8,128)(2,1)} %transfer.1, bf16[192,4096]{1,0:T(8,128)(2,1)} %first.1, bf16[96,4096]{1,0:T(8,128)(2,1)} %second.1, ...), custom_call_target="tpu_custom_call" | custom-call | flops 600000000 | bytes 13000000 | tf_op jit(solution)/shard_map/operator/pallas_call | solution.py:485
  43.5 2.3 %copy.18 = f32[32,8192]{1,0:T(8,128)} copy(f32[32,8192]{1,0:T(8,128)} %operator.1) | data formatting | bytes 2097152

commit v2 on v1

--- a/solution.py
+++ b/solution.py
@@ -34,7 +34,12 @@
 
 def kernel(
     dims,
-    idx,
+    near_at,
+    first_at,
+    second_at,
+    third_at,
+    near_live,
+    couple_live,
     sources,
     basis,
     near,
@@ -99,9 +104,9 @@
 
     loads = []
     pairs = (
-        (transfer, vt),
         (sources, xs.at[:, pl.ds(wide, own)]),
         (basis, vb),
+        (transfer, vt),
         (fold, vf),
         (top, vtop),
         (first, v1),
@@ -165,7 +170,29 @@
         else:
             lax.fori_loop(0, n // width, body, 0)
 
+    every = leaves + 2 * REACH
+    xl[every] = jnp.zeros((columns, points), BF)
+    coefs = (cp0, cp1, cp2)
+    for j, ref in enumerate(coefs):
+        ref[(leaves >> j) + 2 * HALO] = jnp.zeros((columns, rank), BF)
+
     loads[0].wait()
+    loads[1].wait()
+
+    def leaf_body(q, carry):
+        vals = []
+        for u in range(8):
+            leaf = q * 8 + u
+            x = xs[:, pl.ds(pl.multiple_of(wide + leaf * points, points), points)]
+            vals.append(dot_nt(x, vb[leaf]).astype(BF))
+        mixed = dot_nn(jnp.concatenate(vals, axis=0), small).astype(BF)
+        for u in range(8):
+            cp0[HALO + q * 8 + u] = mixed[u * columns : (u + 1) * columns]
+        return carry
+
+    lax.fori_loop(0, leaves // 8, leaf_body, 0)
+
+    loads[2].wait()
     relay(vt, ft)
 
     def put_wt(s, value):
@@ -197,28 +224,6 @@
     for copy in halo:
         copy.start()
 
-    every = leaves + 2 * REACH
-    xl[every] = jnp.zeros((columns, points), BF)
-    coefs = (cp0, cp1, cp2)
-    for j, ref in enumerate(coefs):
-        ref[(leaves >> j) + 2 * HALO] = jnp.zeros((columns, rank), BF)
-
-    loads[1].wait()
-    loads[2].wait()
-
-    def leaf_body(q, carry):
-        vals = []
-        for u in range(8):
-            leaf = q * 8 + u
-            x = xs[:, pl.ds(pl.multiple_of(wide + leaf * points, points), points)]
-            vals.append(dot_nt(x, vb[leaf]).astype(BF))
-        mixed = dot_nn(jnp.concatenate(vals, axis=0), small).astype(BF)
-        for u in range(8):
-            cp0[HALO + q * 8 + u] = mixed[u * columns : (u + 1) * columns]
-        return carry
-
-    lax.fori_loop(0, leaves // 8, leaf_body, 0)
-
     high_start = {}
     position = 0
     for j in range(COUPLED, depth + 1):
@@ -234,9 +239,9 @@
         row = 2 * leaves - 2 * (leaves >> j)
 
         def up(n, src=src, src_at=src_at, row=row):
-            a = dot_nn(src[src_at + 2 * n], wt[row + 2 * n])
-            b = dot_nn(src[src_at + 2 * n + 1], wt[row + 2 * n + 1])
-            return (a + b).astype(BF)
+            pair = jnp.concatenate([src[src_at + 2 * n], src[src_at + 2 * n + 1]], axis=1)
+            both = wt[pl.ds(row + 2 * n, 2)].reshape(2 * rank, rank)
+            return dot_nn(pair, both).astype(BF)
 
         def put(n, value, dst=dst, dst_at=dst_at):
             dst[dst_at + n] = value
@@ -279,6 +284,12 @@
     relay(vf, ff)
     loads[4].wait()
     relay(vtop, ftop)
+    loads[5].wait()
+    relay(v1, f1)
+    loads[6].wait()
+    relay(v2, f2)
+    loads[7].wait()
+    relay(v3, f3)
 
     for copy in sub_copies:
         copy.wait()
@@ -309,32 +320,28 @@
     for copy in leaf_copies:
         copy.start()
 
-    loads[5].wait()
-    relay(v1, f1)
-    loads[6].wait()
-    relay(v2, f2)
-    loads[7].wait()
-    relay(v3, f3)
     for copy in coef_copies:
         copy.wait()
-    base = 3 * leaves
-    for j, (mats, field) in enumerate(((f1, g0), (f2, g1), (f3, g2))):
+    levels = ((f1, g0, first_at), (f2, g1, second_at), (f3, g2, third_at))
+    for j, (mats, field, at) in enumerate(levels):
         n = leaves >> j
         ref = coefs[j]
 
-        def couple(i, n=n, ref=ref, mats=mats, base=base):
-            total = None
+        live = couple_live[0, j]
+
+        def couple(i, n=n, ref=ref, mats=mats, at=at, live=live):
+            rows, cols = [], []
             for t in range(3):
                 s = t * n + i
-                value = dot_nn(ref[idx[base + s]], matrix(mats, s))
-                total = value if total is None else total + value
-            return total
+                node = jnp.where(s < live, at[1, s] - (me * n - HALO), n + 2 * HALO)
+                rows.append(ref[node])
+                cols.append(matrix(mats, s))
+            return dot_nn(jnp.concatenate(rows, axis=1), jnp.concatenate(cols, axis=0))
 
         def put_field(i, value, field=field):
             field[i] = value
 
         blocks(n, 8, couple, put_field)
-        base += 3 * n
 
     for copy in halo:
         copy.wait()
@@ -349,12 +356,16 @@
 
     blocks(every, 8, load_leaf, put_leaf)
 
+    alive = near_live[0]
+
     def near_leaf(leaf):
-        total = None
+        rows, cols = [], []
         for t in range(3):
-            value = dot_nt(xl[idx[t * leaves + leaf]], vn[t, leaf])
-            total = value if total is None else total + value
-        return total
+            s = t * leaves + leaf
+            place_of = jnp.where(s < alive, near_at[1, s] - (me * leaves - REACH), every)
+            rows.append(xl[place_of])
+            cols.append(vn[t, leaf])
+        return dot_nt(jnp.concatenate(rows, axis=1), jnp.concatenate(cols, axis=1))
 
     def put_near(leaf, value):
         out[:, pl.ds(pl.multiple_of(leaf * points, points), points)] = value
@@ -384,16 +395,19 @@
         row = 2 * leaves - 2 * (leaves >> j)
         src_at, dst_at = down_start[j + 1], down_start[j]
 
-        def descend(c, row=row, src_at=src_at, j=j):
-            value = dot_nt(dn[src_at + c // 2], wt[row + c])
+        def descend(n, row=row, src_at=src_at, j=j):
+            both = wt[pl.ds(row + 2 * n, 2)].reshape(2 * rank, rank)
+            value = dot_nt(dn[src_at + n], both)
+            value = (value[:, :rank], value[:, rank:])
             if j < COUPLED:
-                value = value + fields[j][c]
-            return value.astype(BF)
-
-        def put_down(c, value, dst_at=dst_at):
-            dn[dst_at + c] = value
-
-        blocks(leaves >> j, 8, descend, put_down)
+                value = (value[0] + fields[j][2 * n], value[1] + fields[j][2 * n + 1])
+            return value
+
+        def put_down(n, value, dst_at=dst_at):
+            dn[dst_at + 2 * n] = value[0].astype(BF)
+            dn[dst_at + 2 * n + 1] = value[1].astype(BF)
+
+        blocks(leaves >> (j + 1), 8, descend, put_down)
 
     def final_body(q, carry):
         rows = jnp.concatenate([dn[down_start[0] + q * 8 + u] for u in range(8)], axis=0)
@@ -430,17 +444,6 @@
     leaves, rank, points = leaf_basis.shape
     groups = lax.axis_size("leaf")
     members = lax.axis_size("sub")
-    device = lax.axis_index(("leaf", "sub"))
-
-    def slots(index, live, first_node, dead):
-        n = index.shape[0]
-        return jnp.where(lax.iota(jnp.int32, n) < live, index[:, 1] - first_node, dead)
-
-    lists = [slots(near_index, near_count[0], device * leaves - REACH, leaves + 2 * REACH)]
-    for j, index in enumerate((index_first, index_second, index_third)):
-        n = leaves >> j
-        lists.append(slots(index, couple_count[0, j], device * n - HALO, n + 2 * HALO))
-    idx = jnp.concatenate(lists)
 
     near = near_blocks.reshape(3, leaves, points, points)
     top = top_couple.reshape(groups, rank * rank)
@@ -485,7 +488,7 @@
     return pl.pallas_call(
         functools.partial(kernel, dims),
         out_shape=jax.ShapeDtypeStruct((columns, leaves * points), F32),
-        in_specs=[pl.BlockSpec(memory_space=pltpu.SMEM)] + [anywhere] * 9,
+        in_specs=[pl.BlockSpec(memory_space=pltpu.SMEM)] * 6 + [anywhere] * 9,
         out_specs=pl.BlockSpec(memory_space=pltpu.VMEM),
         scratch_shapes=scratch,
         compiler_params=pltpu.CompilerParams(
@@ -496,7 +499,12 @@
         ),
         name="operator",
     )(
-        idx,
+        near_index.T,
+        index_first.T,
+        index_second.T,
+        index_third.T,
+        near_count,
+        couple_count,
         sources,
         leaf_basis,
         near,

time: 46.1 us -> 36.9 us (0.80)
  other arithmetic: 5.32 us -> 0 us
  Pallas kernels: 36.1 us -> 33.8 us
  local copies, waits for them, and re-layouts: 3.68 us -> 2.26 us
    select_n x3 -> x0, other arithmetic: 3.28 us -> none  [slots(): jnp.where(lax.iota(jnp.int32, n) < live, index[:, 1] - first_node, dead)]
    pallas_call x1, Pallas kernels: 36.1 us -> 33.8 us  [local(): pl.pallas_call(functools.partial(kernel, dims), out_shape=jax.ShapeDtypeS...]
    slice x1 -> x0, local copies, waits for them, and re-layouts: 1.41 us -> none  [local(): couple_count[0, j]]
    sub x2 -> x0, other arithmetic: 1.37 us -> none  [slots(): index[:, 1] - first_node]
    concatenate x1 -> x0, other arithmetic: 0.67 us -> none  [local(): idx = jnp.concatenate(lists)]
where the time goes in v2:
time: 36.9 us; the launch traced here: 36.7 us
  Pallas kernels  33.8 us (92%)
  local copies, waits for them, and re-layouts  2.26 us (6%)
  between operations  0.66 us (2%)
    pallas_call x1, Pallas kernels, local(): pl.pallas_call(functools.partial(kernel, dims), out_shape=jax.ShapeDtypeS...  33.8 us
    unnamed x1, local copies, waits for them, and re-layouts  2.26 us

profile of v2, /device:TPU:0, one launch (start us, length us, event | category | flops | bytes accessed | tf_op | source)
XLA Modules:
  0.0 36.7 jit_solution(13324352119480667843)
XLA Ops:
  0.7 33.8 %operator.1 = f32[32,8192]{1,0:T(8,128)} custom-call(s32[2,192]{1,0:T(2,128)} %bitcast.8, s32[2,192]{1,0:T(2,128)} %bitcast.9, s32[2,96]{1,0:T(2,128)} %bitcast.10, s32[2,48]{1,0:T(2,128)} %bitcast.11, s32[1]{0:T(128)S(6)} %copy.17.near_live, s32[1,3]{1,0:T(1,128)} %couple_live.1, bf16[32,8192]{1,0:T(8,128)(2,1)} %sources.1, bf16[64,64,128]{2,1,0:T(8,128)(2,1)} %basis.1, ...), custom_call_target="tpu_custom_call" | custom-call | flops 600000000 | bytes 13000000 | tf_op jit(solution)/shard_map/operator/pallas_call | solution.py:488
  34.5 2.3 %copy.18 = f32[32,8192]{1,0:T(8,128)} copy(f32[32,8192]{1,0:T(8,128)} %operator.1) | data formatting | bytes 2097152

commit v3 on v2

--- a/solution.py
+++ b/solution.py
@@ -138,7 +138,7 @@
 
     def relay(src, dst):
         rows = src.shape[0]
-        step = 8
+        step = 16
 
         def body(q, carry):
             vals = []
@@ -246,7 +246,7 @@
         def put(n, value, dst=dst, dst_at=dst_at):
             dst[dst_at + n] = value
 
-        blocks(leaves >> (j + 1), 8, up, put)
+        blocks(leaves >> (j + 1), 32, up, put)
 
     root = 2 * leaves - 2
     terms[sb] = dot_nn(chi[high_start[depth]], wt[root])
@@ -341,7 +341,7 @@
         def put_field(i, value, field=field):
             field[i] = value
 
-        blocks(n, 8, couple, put_field)
+        blocks(n, 32, couple, put_field)
 
     for copy in halo:
         copy.wait()
@@ -370,7 +370,7 @@
     def put_near(leaf, value):
         out[:, pl.ds(pl.multiple_of(leaf * points, points), points)] = value
 
-    blocks(leaves, 8, near_leaf, put_near)
+    blocks(leaves, 32, near_leaf, put_near)
 
     for copy in leaf_copies:
         copy.wait()
@@ -407,20 +407,20 @@
             dn[dst_at + 2 * n] = value[0].astype(BF)
             dn[dst_at + 2 * n + 1] = value[1].astype(BF)
 
-        blocks(leaves >> (j + 1), 8, descend, put_down)
+        blocks(leaves >> (j + 1), 32, descend, put_down)
 
     def final_body(q, carry):
-        rows = jnp.concatenate([dn[down_start[0] + q * 8 + u] for u in range(8)], axis=0)
+        rows = jnp.concatenate([dn[down_start[0] + q * 16 + u] for u in range(16)], axis=0)
         natural = dot_nt(rows, small).astype(BF)
-        for u in range(8):
-            leaf = q * 8 + u
+        for u in range(16):
+            leaf = q * 16 + u
             at = pl.ds(pl.multiple_of(leaf * points, points), points)
             out[:, at] = out[:, at] + dot_nn(
                 natural[u * columns : (u + 1) * columns], vb[leaf]
             )
         return carry
 
-    lax.fori_loop(0, leaves // 8, final_body, 0)
+    lax.fori_loop(0, leaves // 16, final_body, 0)
 
 
 def local(

time: 36.9 us -> 31.3 us (0.85)
  Pallas kernels: 33.8 us -> 28.2 us
    pallas_call x1, Pallas kernels: 33.8 us -> 28.2 us  [local(): pl.pallas_call(functools.partial(kernel, dims), out_shape=jax.ShapeDtypeS...]
where the time goes in v3:
time: 31.3 us; the launch traced here: 31.1 us
  Pallas kernels  28.2 us (90%)
  local copies, waits for them, and re-layouts  2.26 us (7%)
  between operations  0.66 us (2%)
    pallas_call x1, Pallas kernels, local(): pl.pallas_call(functools.partial(kernel, dims), out_shape=jax.ShapeDtypeS...  28.2 us
    unnamed x1, local copies, waits for them, and re-layouts  2.26 us

profile of v3, /device:TPU:0, one launch (start us, length us, event | category | flops | bytes accessed | tf_op | source)
XLA Modules:
  0.0 31.1 jit_solution(5768679763775181984)
XLA Ops:
  0.7 28.2 %operator.1 = f32[32,8192]{1,0:T(8,128)} custom-call(s32[2,192]{1,0:T(2,128)} %bitcast.8, s32[2,192]{1,0:T(2,128)} %bitcast.9, s32[2,96]{1,0:T(2,128)} %bitcast.10, s32[2,48]{1,0:T(2,128)} %bitcast.11, s32[1]{0:T(128)S(6)} %copy.17.near_live, s32[1,3]{1,0:T(1,128)} %couple_live.1, bf16[32,8192]{1,0:T(8,128)(2,1)} %sources.1, bf16[64,64,128]{2,1,0:T(8,128)(2,1)} %basis.1, ...), custom_call_target="tpu_custom_call" | custom-call | flops 600000000 | bytes 13000000 | tf_op jit(solution)/shard_map/operator/pallas_call | solution.py:488
  28.9 2.3 %copy.18 = f32[32,8192]{1,0:T(8,128)} copy(f32[32,8192]{1,0:T(8,128)} %operator.1) | data formatting | bytes 2097152
